TPU v7x, 128 devices: a whole 4x4x4 slice. The times are simulated.
128 devices in a mesh: ty: 16 (over x_hi, y, core), tx: 8 (over x_lo, z).
Axes of the slice: x: 4 (x_hi: 2, x_lo: 2; x = x_hi * 2 + x_lo), y: 4, z: 4, core: 2. Of those that a mesh axis runs over, the one named last changes fastest.
Arguments:
- spectrum: float32 [2, 8192, 8192], P(None, 'ty', 'tx'), may hold values from -6 to 6
- pupil: float32 [2, 512, 512], replicated, may hold values from -6 to 6
- amplitudes: float32 [384, 512, 512], P(('ty', 'tx')), may hold values from 0 to 3
- offsets: int32 [384, 2], P(('ty', 'tx')), may hold values from 0 to 7680, as said below
- live: int32 [384], P(('ty', 'tx')), may hold values from 0 to 1, as said below
Outputs:
- spectrum_grad: float32 [2, 8192, 8192], P(None, 'ty', 'tx')
- pupil_grad: float32 [2, 512, 512], replicated
Inputs may be any that keep to these rules, and one draw needn't show every extreme that they name: `offsets`: the slots of the device at ty index i and tx index j are i * 8 * 3 + j * 3 to that plus 3 - 1; each such slot's corner has row in [i * 512, (i + 1) * 512) and column in [j * 1024, (j + 1) * 1024), and its window lies inside the spectrum. Each device's live slots come first among its 3 slots, and every device has at least one. Two devices with the same tx index whose ty indices differ by 8 hold together at most 4 live slots; some such pair holds exactly that many, and some device has all 3 slots live.
All inputs are finite; a program needn't handle non-finite values.
Results may differ from a plain program's by a relative error of at most 0.0001.
Values sent between devices are 32-bit elements; how exact they have to be, the bound alone decides.
A program may use at most 192 MiB of HBM per device.

v0:
```python
import math

import jax
import jax.numpy as jnp
from jax import lax
from jax.sharding import PartitionSpec as P

exact_mode = lax.Precision.HIGHEST


def from_behind(array, axis, by):
    devices = lax.axis_size(axis)
    pairs = [(i, i + by) for i in range(devices) if 0 <= i + by < devices]
    return lax.ppermute(array, axis, pairs)


def dft_tables(length):
    indices = jnp.arange(length, dtype=jnp.int32)
    phases = indices[:, None] * indices[None, :] % length
    angles = phases.astype(jnp.float32) * (2.0 * math.pi / length)
    factor = 1.0 / math.sqrt(length)
    return (jnp.cos(angles) * factor, -jnp.sin(angles) * factor)


def left_product(mat_re, mat_im, val_re, val_im):
    out_re = jnp.einsum("km,smn->skn", mat_re, val_re, precision=exact_mode) - jnp.einsum(
        "km,smn->skn", mat_im, val_im, precision=exact_mode
    )
    out_im = jnp.einsum("km,smn->skn", mat_re, val_im, precision=exact_mode) + jnp.einsum(
        "km,smn->skn", mat_im, val_re, precision=exact_mode
    )
    return (out_re, out_im)


def right_product(val_re, val_im, mat_re, mat_im):
    out_re = jnp.einsum("smn,nk->smk", val_re, mat_re, precision=exact_mode) - jnp.einsum(
        "smn,nk->smk", val_im, mat_im, precision=exact_mode
    )
    out_im = jnp.einsum("smn,nk->smk", val_re, mat_im, precision=exact_mode) + jnp.einsum(
        "smn,nk->smk", val_im, mat_re, precision=exact_mode
    )
    return (out_re, out_im)


def led_terms(windows, measured, pupil, weights):
    cosine, sine = dft_tables(measured.shape[-1])
    win_re = windows[:, 0]
    win_im = windows[:, 1]
    pup_re = pupil[0]
    pup_im = pupil[1]
    prod_re = win_re * pup_re - win_im * pup_im
    prod_im = win_re * pup_im + win_im * pup_re
    half_re, half_im = left_product(cosine, -sine, prod_re, prod_im)
    field_re, field_im = right_product(half_re, half_im, cosine, -sine)
    modulus = jnp.sqrt(field_re * field_re + field_im * field_im + 1.0)
    factor = 1.0 - measured / modulus
    half_re, half_im = left_product(cosine, sine, factor * field_re, factor * field_im)
    back_re, back_im = right_product(half_re, half_im, cosine, sine)
    masks = weights[:, None, None]
    dwin_re = (pup_re * back_re + pup_im * back_im) * masks
    dwin_im = (pup_re * back_im - pup_im * back_re) * masks
    dpup_re = jnp.sum((win_re * back_re + win_im * back_im) * masks, axis=0)
    dpup_im = jnp.sum((win_re * back_im - win_im * back_re) * masks, axis=0)
    return (jnp.stack([dwin_re, dwin_im], axis=1), jnp.stack([dpup_re, dpup_im], axis=0))


def cut_windows(region, rows_local, cols_local, window):
    zero_idx = jnp.zeros((), jnp.int32)
    pieces = [
        lax.dynamic_slice(
            region, (zero_idx, rows_local[number], cols_local[number]), (2, window, window)
        )
        for number in range(rows_local.shape[0])
    ]
    return jnp.stack(pieces, axis=0)


def place_windows(grads, rows_local, cols_local, shape):
    zero_idx = jnp.zeros((), jnp.int32)
    window = grads.shape[-1]
    region = jnp.zeros(shape, jnp.float32)
    for number in range(grads.shape[0]):
        start = (zero_idx, rows_local[number], cols_local[number])
        current = lax.dynamic_slice(region, start, (2, window, window))
        region = lax.dynamic_update_slice(region, current + grads[number], start)
    return region


def body(spectrum, pupil, amplitudes, offsets, live):
    window = pupil.shape[-1]
    tile_rows = spectrum.shape[1]
    tile_cols = spectrum.shape[2]
    rows_local = offsets[:, 0] - lax.axis_index("ty") * tile_rows
    cols_local = offsets[:, 1] - lax.axis_index("tx") * tile_cols
    right_strip = from_behind(spectrum[:, :, :window], "tx", -1)
    widened = jnp.concatenate([spectrum, right_strip], axis=2)
    lower_strip = from_behind(widened, "ty", -1)
    region = jnp.concatenate([widened, lower_strip], axis=1)
    windows = cut_windows(region, rows_local, cols_local, window)
    weights = live.astype(jnp.float32)
    dwin, dpup = led_terms(windows, amplitudes, pupil, weights)
    grad_region = place_windows(dwin, rows_local, cols_local, region.shape)
    back_lower = from_behind(grad_region[:, tile_rows:, :], "ty", 1)
    wide_grad = grad_region[:, :tile_rows, :].at[:, :window, :].add(back_lower)
    back_right = from_behind(wide_grad[:, :, tile_cols:], "tx", 1)
    spec_grad = wide_grad[:, :, :tile_cols].at[:, :, :window].add(back_right)
    pupil_total = lax.psum(dpup, ("ty", "tx"))
    norm_scale = 1.0 / math.sqrt(lax.axis_size("ty") * lax.axis_size("tx"))
    return (spec_grad, pupil_total * norm_scale)


def solution(mesh):
    return jax.shard_map(
        body,
        mesh=mesh,
        in_specs=(
            P(None, "ty", "tx"),
            P(),
            P(("ty", "tx"), None, None),
            P(("ty", "tx"), None),
            P(("ty", "tx")),
        ),
        out_specs=(P(None, "ty", "tx"), P()),
        check_vma=False,
    )
```

profile of v0, /device:TPU:1, one launch (start us, length us, event | category | flops | bytes accessed | tf_op | source)
XLA Modules:
  0.0 687.4 jit_solution(5432926706804704480)
XLA Ops:
  12.8 46.1 %collective-permute-done = f32[2,512,512]{2,1,0:T(8,128)S(1)} collective-permute-done((f32[2,512,512]{2,1,0:T(8,128)S(1)}, f32[2,512,512]{2,1,0:T(8,128)S(1)}, u32[]{:S(2)}, u32[]{:S(2)}) %collective-permute-start) | collective-permute-done | bytes 2097184 | tf_op jit(solution)/shard_map/ppermute | solution.py:14
  60.4 3.1 collective-permute-start.1
  76.1 57.6 %collective-permute-done.1 = f32[2,512,1536]{2,1,0:T(8,128)} collective-permute-done((f32[2,512,1536]{2,1,0:T(8,128)}, f32[2,512,1536]{2,1,0:T(8,128)}, u32[]{:S(2)}, u32[]{:S(2)}) %collective-permute-start.1) | collective-permute-done | bytes 6291488 | tf_op jit(solution)/shard_map/ppermute | solution.py:14
  133.7 6.9 %fusion.26 = (f32[1,2,512,512]{3,2,0,1:T(8,128)S(1)}, f32[1,2,512,512]{3,2,0,1:T(8,128)S(1)}, f32[1,2,512,512]{3,2,0,1:T(8,128)S(1)}) fusion(s32[]{:T(128)S(6)} %select_n.65, s32[]{:T(128)S(6)} %select_n.66, f32[2,512,1536]{2,1,0:T(8,128)} %constant_dynamic-update-slice_fusion, f32[2,512,1536]{2,1,0:T(8,128)} %collective-permute-done.1, s32[]{:T(128)S(6)} %select_n.67, ...), kind=kLoop, calls=%fused_computation.47 | loop fusion | flops 1572864 | bytes 18874392 | tf_op jit(solution)/shard_map/stack | solution.py:75
  142.0 14.7 %fusion.53 = f32[3,512,512]{2,1,0:T(8,128)S(1)} fusion(f32[3,2,512,512]{3,2,0,1:T(8,128)S(1)} %pad_maximum_fusion, f32[512,512]{1,0:T(8,128)S(1)} %get-tuple-element.44, f32[512,512]{1,0:T(8,128)S(1)} %get-tuple-element.43), kind=kOutput, calls=%fused_computation.76 | convolution fusion | flops 4838653952 | bytes 11534336 | tf_op jit(solution)/shard_map/km,smn->skn/dot_general | solution.py:29
  156.6 14.4 %convolution_add_fusion.1 = f32[3,512,512]{2,1,0:T(8,128)S(1)} fusion(f32[3,512,512]{2,1,0:T(8,128)S(1)} %fusion.53, f32[3,2,512,512]{3,2,0,1:T(8,128)S(1)} %pad_maximum_fusion, f32[512,512]{1,0:T(8,128)S(1)} %get-tuple-element.44, f32[512,512]{1,0:T(8,128)S(1)} %get-tuple-element.43), kind=kOutput, calls=%fused_computation.62 | convolution fusion | flops 4838916096 | bytes 14680064 | tf_op jit(solution)/shard_map/km,smn->skn/dot_general | solution.py:29
  171.0 9.3 %fusion.8 = f32[3,512,512]{2,1,0:T(8,128)S(1)} fusion(f32[3,512,512]{2,1,0:T(8,128)S(1)} %convolution_add_fusion.1), kind=kOutput, calls=%fused_computation.22 | convolution fusion | flops 4835770368 | bytes 6291456 | tf_op jit(solution)/shard_map/smn,nk->smk/dot_general | solution.py:39
  180.3 9.6 %fusion.10 = f32[3,512,512]{2,1,0:T(8,128)S(1)} fusion(f32[3,512,512]{2,1,0:T(8,128)S(1)} %convolution_add_fusion.1), kind=kOutput, calls=%fused_computation.24 | convolution fusion | flops 4836294656 | bytes 6291456 | tf_op jit(solution)/shard_map/smn,nk->smk/dot_general | solution.py:36
  190.0 14.4 %fusion.55 = f32[3,512,512]{2,1,0:T(8,128)S(1)} fusion(f32[3,2,512,512]{3,2,0,1:T(8,128)S(1)} %pad_maximum_fusion, f32[512,512]{1,0:T(8,128)S(1)} %get-tuple-element.44, f32[512,512]{1,0:T(8,128)S(1)} %get-tuple-element.43), kind=kOutput, calls=%fused_computation.78 | convolution fusion | flops 4838653952 | bytes 11534336 | tf_op jit(solution)/shard_map/km,smn->skn/dot_general | solution.py:26
  204.4 14.4 %convolution_subtract_fusion.1 = f32[3,512,512]{2,1,0:T(8,128)S(1)} fusion(f32[3,512,512]{2,1,0:T(8,128)S(1)} %fusion.55, f32[3,2,512,512]{3,2,0,1:T(8,128)S(1)} %pad_maximum_fusion, f32[512,512]{1,0:T(8,128)S(1)} %get-tuple-element.44, f32[512,512]{1,0:T(8,128)S(1)} %get-tuple-element.43), kind=kOutput, calls=%fused_computation.63 | convolution fusion | flops 4838916096 | bytes 14680064 | tf_op jit(solution)/shard_map/km,smn->skn/dot_general | solution.py:26
  218.8 9.7 %fusion.35 = f32[3,512,512]{2,1,0:T(8,128)S(1)} fusion(f32[3,512,512]{2,1,0:T(8,128)S(1)} %fusion.8, f32[3,512,512]{2,1,0:T(8,128)S(1)} %convolution_subtract_fusion.1), kind=kOutput, calls=%fused_computation.57 | convolution fusion | flops 4837081088 | bytes 9437184 | tf_op jit(solution)/shard_map/smn,nk->smk/dot_general | solution.py:39
  228.5 9.4 %fusion.32 = f32[3,512,512]{2,1,0:T(8,128)S(1)} fusion(f32[3,512,512]{2,1,0:T(8,128)S(1)} %fusion.10, f32[3,512,512]{2,1,0:T(8,128)S(1)} %convolution_subtract_fusion.1), kind=kOutput, calls=%fused_computation.56 | convolution fusion | flops 4836556800 | bytes 9437184 | tf_op jit(solution)/shard_map/smn,nk->smk/dot_general | solution.py:36
  237.9 14.7 %fusion.58 = f32[3,512,512]{2,1,0:T(8,128)S(1)} fusion(f32[3,512,512]{2,1,0:T(8,128)S(1)} %fusion.35, f32[3,512,512]{2,1,0:T(8,128)S(1)} %copy-done.5, f32[3,512,512]{2,1,0:T(8,128)S(1)} %fusion.32), kind=kOutput, calls=%fused_computation.81 | convolution fusion | flops 4841275392 | bytes 12582912 | tf_op jit(solution)/shard_map/km,smn->skn/dot_general | solution.py:29
  252.7 15.1 %convolution_add_fusion = f32[3,512,512]{2,1,0:T(8,128)S(1)} fusion(f32[3,512,512]{2,1,0:T(8,128)S(1)} %fusion.58, f32[3,512,512]{2,1,0:T(8,128)S(1)} %fusion.32, f32[3,512,512]{2,1,0:T(8,128)S(1)} %copy-done.5, f32[3,512,512]{2,1,0:T(8,128)S(1)} %fusion.35), kind=kOutput, calls=%fused_computation.60 | convolution fusion | flops 4842323968 | bytes 15728640 | tf_op jit(solution)/shard_map/km,smn->skn/dot_general | solution.py:29
  267.7 9.3 %fusion = f32[3,512,512]{2,1,0:T(8,128)S(1)} fusion(f32[3,512,512]{2,1,0:T(8,128)S(1)} %convolution_add_fusion), kind=kOutput, calls=%fused_computation.14 | convolution fusion | flops 4835770368 | bytes 6291456 | tf_op jit(solution)/shard_map/smn,nk->smk/dot_general | solution.py:39
  277.0 15.9 %fusion.2 = f32[3,512,512]{2,1,0:T(8,128)} fusion(f32[3,512,512]{2,1,0:T(8,128)S(1)} %convolution_add_fusion), kind=kOutput, calls=%fused_computation.16 | convolution fusion | flops 4836032512 | bytes 6291456 | tf_op jit(solution)/shard_map/smn,nk->smk/dot_general | solution.py:36
  293.0 14.7 %fusion.61 = f32[3,512,512]{2,1,0:T(8,128)S(1)} fusion(f32[3,512,512]{2,1,0:T(8,128)S(1)} %fusion.32, f32[3,512,512]{2,1,0:T(8,128)S(1)} %copy-done.5, f32[3,512,512]{2,1,0:T(8,128)S(1)} %fusion.35), kind=kOutput, calls=%fused_computation.84 | convolution fusion | flops 4841275392 | bytes 12582912 | tf_op jit(solution)/shard_map/km,smn->skn/dot_general | solution.py:26
  307.7 14.8 %convolution_subtract_fusion = f32[3,512,512]{2,1,0:T(8,128)S(1)} fusion(f32[3,512,512]{2,1,0:T(8,128)S(1)} %fusion.61, f32[3,512,512]{2,1,0:T(8,128)S(1)} %fusion.35, f32[3,512,512]{2,1,0:T(8,128)S(1)} %copy-done.5, f32[3,512,512]{2,1,0:T(8,128)S(1)} %fusion.32), kind=kOutput, calls=%fused_computation.61 | convolution fusion | flops 4842323968 | bytes 15728640 | tf_op jit(solution)/shard_map/km,smn->skn/dot_general | solution.py:26
  322.5 9.7 %fusion.41 = f32[3,512,512]{2,1,0:T(8,128)S(1)} fusion(f32[3,512,512]{2,1,0:T(8,128)S(1)} %fusion, f32[3,512,512]{2,1,0:T(8,128)S(1)} %convolution_subtract_fusion), kind=kOutput, calls=%fused_computation.59 | convolution fusion | flops 4836818944 | bytes 9437184 | tf_op jit(solution)/shard_map/smn,nk->smk/dot_general | solution.py:39
  332.2 20.4 %multiply_reduce_fusion.1 = (f32[512,512]{1,0:T(8,128)}, f32[512,512]{1,0:T(8,128)}, f32[3,1,512,512]{3,2,0,1:T(8,128)S(1)}, f32[3,1,512,512]{3,2,0,1:T(8,128)S(1)}) fusion(f32[3,512,512]{2,1,0:T(8,128)S(1)} %fusion.41, f32[3,2,512,512]{3,2,0,1:T(8,128)S(1)} %pad_maximum_fusion, f32[3]{0:T(128)S(1)} %convert_element_type.37, ...), kind=kOutput, calls=%fused_computation.31 | convolution fusion | flops 4850188288 | bytes 26214412 | tf_op jit(solution)/shard_map/smn,nk->smk/dot_general | solution.py:36
  355.0 6.1 broadcast_in_dim.2
  361.1 14.7 %dynamic_update_slice.9 = f32[2,1024,1536]{2,1,0:T(8,128)} dynamic-update-slice(f32[2,1024,1536]{2,1,0:T(8,128)} %broadcast_in_dim.2, f32[2,512,512]{2,1,0:T(8,128)} %fusion.22, s32[]{:T(128)} %constant.90.clone.1, s32[]{:T(128)S(6)} %select_n.65, s32[]{:T(128)S(6)} %select_n.66) | dynamic-update-slice | bytes 4194308 | tf_op jit(solution)/shard_map/dynamic_update_slice | solution.py:85
  375.8 4.0 fusion.20
  379.8 15.1 %dynamic_update_slice.10 = f32[2,1024,1536]{2,1,0:T(8,128)} dynamic-update-slice(f32[2,1024,1536]{2,1,0:T(8,128)} %dynamic_update_slice.9, f32[2,512,512]{2,1,0:T(8,128)} %fusion.20, s32[]{:T(128)} %constant.90.clone.1, s32[]{:T(128)S(6)} %select_n.67, s32[]{:T(128)S(6)} %select_n.68) | dynamic-update-slice | bytes 4194308 | tf_op jit(solution)/shard_map/dynamic_update_slice | solution.py:85
  394.9 4.0 fusion.31
  399.0 15.1 %dynamic_update_slice.11 = f32[2,1024,1536]{2,1,0:T(8,128)} dynamic-update-slice(f32[2,1024,1536]{2,1,0:T(8,128)} %dynamic_update_slice.10, f32[2,512,512]{2,1,0:T(8,128)} %fusion.31, s32[]{:T(128)} %constant.90.clone.1, s32[]{:T(128)S(6)} %select_n.69, s32[]{:T(128)S(6)} %select_n.70) | dynamic-update-slice | bytes 4194308 | tf_op jit(solution)/shard_map/dynamic_update_slice | solution.py:85
  414.0 3.4 slice.144
  420.1 67.9 %collective-permute-done.2 = f32[2,512,1536]{2,1,0:T(8,128)} collective-permute-done((f32[2,512,1536]{2,1,0:T(8,128)S(1)}, f32[2,512,1536]{2,1,0:T(8,128)}, u32[]{:S(2)}, u32[]{:S(2)}) %collective-permute-start.2) | collective-permute-done | bytes 6291488 | tf_op jit(solution)/shard_map/ppermute | solution.py:14
  488.0 4.2 slice_add_fusion
  496.3 3.0 collective-permute-start.3
  500.9 171.3 %all-reduce.2.cloned.1.call-done = f32[2,512,512]{2,1,0:T(8,128)} async-done(((f32[2,512,512]{2,1,0:T(8,128)}), f32[2,512,512]{2,1,0:T(8,128)}) %all-reduce.2.cloned.1.call-update) | async-done | bytes 2097168 | tf_op jit(solution)/shard_map/psum | solution.py:107
  672.2 3.3 broadcast_multiply_fusion
  (43 shorter events, 24.9 us)
Async XLA Ops:
  7.2 665.0 %all-reduce.2.cloned.1.call-start = ((), (), s32[]{:S(2)}) async-start(), calls=%async_computation | async-start | bytes 4194304 | tf_op jit(solution)/shard_map/psum | solution.py:107
  7.2 3.2 copy-start.6
  9.1 49.7 %collective-permute-start = (f32[2,512,512]{2,1,0:T(8,128)S(1)}, f32[2,512,512]{2,1,0:T(8,128)S(1)}, u32[]{:S(2)}, u32[]{:S(2)}) collective-permute-start(f32[2,512,512]{2,1,0:T(8,128)S(1)} %slice.117), channel_id=1, source_target_pairs={{1,0},{2,1},{3,2},{4,3},{5,4},{6,5},{7,6},{9,8},{10,9},{11,10},{12... | collective-permute-start | bytes 6291464 | tf_op jit(solution)/shard_map/ppermute | solution.py:14
  12.8 50.8 %copy-start.10 = (s32[3,2]{0,1:T(2,128)S(1)}, s32[3,2]{0,1:T(2,128)}, u32[]{:S(2)}) copy-start(s32[3,2]{0,1:T(2,128)} %param.14) | copy-start | bytes 76
  12.8 59.2 %copy-start.11 = (s32[3]{0:T(128)S(1)}, s32[3]{0:T(128)}, u32[]{:S(2)}) copy-start(s32[3]{0:T(128)} %param.15) | copy-start | bytes 40
  12.8 63.1 %copy-start.9 = (f32[2,512,512]{2,1,0:T(8,128)S(1)}, f32[2,512,512]{2,1,0:T(8,128)}, u32[]{:S(2)}) copy-start(f32[2,512,512]{2,1,0:T(8,128)} %param.12) | copy-start | bytes 6291460
  60.4 73.3 %collective-permute-start.1 = (f32[2,512,1536]{2,1,0:T(8,128)}, f32[2,512,1536]{2,1,0:T(8,128)}, u32[]{:S(2)}, u32[]{:S(2)}) collective-permute-start(f32[2,512,1536]{2,1,0:T(8,128)} %constant_dynamic-update-slice_fusion), channel_id=1, source_target_pairs={{8,0},{16,8},{24,16},{32,24},{40,32},{48,40},{56,48},{64,56},{72,6... | collective-permute-start | bytes 18874376 | tf_op jit(solution)/shard_map/ppermute | solution.py:14
  228.5 9.4 %copy-start.5 = (f32[3,512,512]{2,1,0:T(8,128)S(1)}, f32[3,512,512]{2,1,0:T(8,128)}, u32[]{:S(2)}) copy-start(f32[3,512,512]{2,1,0:T(8,128)} %param.13) | copy-start | bytes 9437188
  352.6 2.4 copy-start.1
  414.0 74.0 %copy-start = (f32[2,1024,1536]{2,1,0:T(8,128)S(1)}, f32[2,1024,1536]{2,1,0:T(8,128)}, u32[]{:S(2)}) copy-start(f32[2,1024,1536]{2,1,0:T(8,128)} %dynamic_update_slice.11) | copy-start | bytes 37748740
  417.4 70.5 %collective-permute-start.2 = (f32[2,512,1536]{2,1,0:T(8,128)S(1)}, f32[2,512,1536]{2,1,0:T(8,128)}, u32[]{:S(2)}, u32[]{:S(2)}) collective-permute-start(f32[2,512,1536]{2,1,0:T(8,128)S(1)} %slice.144), channel_id=1, source_target_pairs={{0,8},{8,16},{16,24},{24,32},{32,40},{40,48},{48,56},{56,64},{64,7... | collective-permute-start | bytes 18874376 | tf_op jit(solution)/shard_map/ppermute | solution.py:14
  492.1 2.7 copy-start.2
  494.8 4.5 copy-start.7
  494.8 4.5 copy-start.8
  496.3 179.2 %collective-permute-start.3 = (f32[2,512,512]{2,1,0:T(8,128)}, f32[2,512,512]{2,1,0:T(8,128)S(1)}, u32[]{:S(2)}, u32[]{:S(2)}) collective-permute-start(f32[2,512,512]{2,1,0:T(8,128)} %slice.147), channel_id=1, source_target_pairs={{0,1},{1,2},{2,3},{3,4},{4,5},{5,6},{6,7},{8,9},{9,10},{10,11},{11... | collective-permute-start | bytes 6291464 | tf_op jit(solution)/shard_map/ppermute | solution.py:14
  672.2 4.2 copy-start.3
  675.5 2.4 slice-start
  678.4 2.0 copy-start.4
Sparse Core Ops, SparseCore 0:
  501.0 171.1 all-reduce.1
where the time goes:
time: 699 us; the launch traced here: 687 us
  waiting for transfers between devices  343 us (49%)
  matrix products  211 us (30%)
  local copies, waits for them, and re-layouts  70.3 us (10%)
  other arithmetic  27.5 us (4%)
  between operations  26.1 us (4%)
  starting transfers between devices  10.1 us (1%)
    ppermute x4, waiting for transfers between devices, from_behind(): return lax.ppermute(array, axis, pairs)  172 us
    psum x1, waiting for transfers between devices, body(): pupil_total = lax.psum(dpup, ('ty', 'tx'))  171 us
    dynamic_update_slice x3, local copies, waits for them, and re-layouts, place_windows(): region = lax.dynamic_update_slice(region, current + grads[number], start)  44.9 us
    dot_general x2, matrix products, right_product(): jnp.einsum('smn,nk->smk', val_re, mat_re, precision=exact_mode)  29.8 us
    dot_general x2, matrix products, left_product(): jnp.einsum('km,smn->skn', mat_im, val_re, precision=exact_mode)  29.7 us
    dot_general x2, matrix products, left_product(): jnp.einsum('km,smn->skn', mat_im, val_im, precision=exact_mode)  29.2 us
    dot_general x2, matrix products, left_product(): jnp.einsum('km,smn->skn', mat_re, val_re, precision=exact_mode)  29.1 us
    dot_general x2, matrix products, left_product(): jnp.einsum('km,smn->skn', mat_re, val_im, precision=exact_mode)  29.1 us
  transfers between devices with their start and end apart: 5, of which 4 were waited for; matrix products, arithmetic and copies ran while one was open for 1% of the time, Pallas kernels for 0%

commit v1 on v0

v1 whole, which is shorter than its diff:
```python
import math
import numpy as np
import ml_dtypes
import jax, jax.numpy as jnp, functools
from jax import lax
from jax.sharding import PartitionSpec as P
from jax.experimental import pallas as pl
from jax.experimental.pallas import tpu as pltpu
F32=jnp.float32; BF=jnp.bfloat16
N_TY = 16
N_TX = 8
M = 512
Q = 128

def tables():
    n=np.arange(Q)[None,:]; k=np.arange(Q)[:,None]
    hi=[];lo=[]
    for q in range(4):
        ang=2*np.pi*((n*(4*k+q))%M)/M
        c=np.cos(ang)/math.sqrt(M); s=np.sin(ang)/math.sqrt(M)
        m=np.block([[c,-s],[s,c]])
        h=m.astype(ml_dtypes.bfloat16); l=(m-h.astype(np.float64)).astype(ml_dtypes.bfloat16)
        hi.append(h); lo.append(l)
    hi=np.stack(hi); lo=np.stack(lo)
    perm=np.zeros((M,M),ml_dtypes.bfloat16)
    for q in range(4):
        for j in range(Q): perm[4*j+q,q*Q+j]=1
    T=lambda a: np.ascontiguousarray(np.swapaxes(a,1,2))
    return hi,lo,T(hi),T(lo),perm

def split(x):
    h=x.astype(BF)
    return h,(x-h.astype(F32)).astype(BF)

def dot(a,b):
    return jnp.dot(a,b,preferred_element_type=F32)

def lmul(mh,ml,y):
    h,l=split(y)
    return dot(jnp.concatenate([mh,ml,mh],axis=1),jnp.concatenate([h,h,l],axis=0))

def rmul(y,mh,ml):
    h,l=split(y)
    return dot(jnp.concatenate([h,l,h],axis=1),jnp.concatenate([mh,mh,ml],axis=0))

def fly_in(xr,xi):
    a=(xr[0]+xr[2],xi[0]+xi[2]); b=(xr[0]-xr[2],xi[0]-xi[2])
    c=(xr[1]+xr[3],xi[1]+xi[3]); d=(xr[1]-xr[3],xi[1]-xi[3])
    return [(a[0]+c[0],a[1]+c[1]),(b[0]-d[1],b[1]+d[0]),(a[0]-c[0],a[1]-c[1]),(b[0]+d[1],b[1]-d[0])]

def fly_out(e):
    a=(e[0][0]+e[2][0],e[0][1]+e[2][1]); b=(e[0][0]-e[2][0],e[0][1]-e[2][1])
    c=(e[1][0]+e[3][0],e[1][1]+e[3][1]); d=(e[1][0]-e[3][0],e[1][1]-e[3][1])
    return [(a[0]+c[0],a[1]+c[1]),(b[0]+d[1],b[1]-d[0]),(a[0]-c[0],a[1]-c[1]),(b[0]-d[1],b[1]+d[0])]

CB=256; RB=256

def rows_from(ref,p,start):
    low=lax.rem(start,8)
    x=ref[p,pl.ds(pl.multiple_of(start-low,8),Q+8),:]
    return pltpu.roll(x,lax.rem(Q+8-low,Q+8),0)[:Q]

def kern2(off, live, X_h, R_h, L_h, C_h, amp_h, pup_h, mh, ml, th, tl, pm, pt, G_h, DP_h,
          X, G, A, AP, PP, PR, W, H, D, DP, sem, osem):
    cps=[]
    for i,(s,d) in enumerate([(pup_h,PP.at[:,0:M]),(pup_h,PP.at[:,M:2*M]),(amp_h,A),
                 (X_h,X.at[:,0:M,0:1024]),(R_h,X.at[:,0:M,1024:1536]),
                 (L_h,X.at[:,M:2*M,0:1024]),(C_h,X.at[:,M:2*M,1024:1536])]):
        cp=pltpu.make_async_copy(s,d,sem.at[i]); cp.start(); cps.append(cp)
    r0=lax.axis_index("ty")*512; c0_=lax.axis_index("tx")*1024
    @pl.loop(0,16)
    def _(i):
        G[:,pl.ds(pl.multiple_of(i*64,64),64),:]=jnp.zeros((2,64,1536),F32)
    DP[...]=jnp.zeros((2,M,M),F32)
    for cp in cps[0:3]: cp.wait()
    @pl.loop(0,3)
    def _(s):
        @pl.when(live[s]>0)
        def _():
            for q in range(2):
                h,l=split(A[s,q*RB:(q+1)*RB,:])
                H[0,q*RB:(q+1)*RB,:]=dot(jnp.concatenate([h,l],axis=1),jnp.concatenate([pm[...],pm[...]],axis=0))
            for q in range(2):
                h,l=split(H[0,:,q*RB:(q+1)*RB])
                AP[s,:,q*RB:(q+1)*RB]=dot(jnp.concatenate([pt[...],pt[...]],axis=1),jnp.concatenate([h,l],axis=0))
    for cp in cps[3:]: cp.wait()
    @pl.loop(0,3)
    def _(s):
        @pl.when(live[s]>0)
        def _():
            r=off[s,0]-r0; c=off[s,1]-c0_
            qc=c//M; c0=c-qc*M
            @pl.loop(0,4)
            def _(b):
                for p in range(2):
                    x=rows_from(PP,p,lax.rem(M-r,M)+b*Q)
                    PR[p,pl.ds(pl.multiple_of(b*Q,Q),Q),:]=pltpu.roll(x,c0,1)
            @pl.loop(0,M//CB)
            def _(j):
                cols=pl.ds(pl.multiple_of(j*CB,CB),CB)
                b1=pl.ds(pl.multiple_of(qc*M+j*CB,CB),CB); b2=pl.ds(pl.multiple_of(qc*M+M+j*CB,CB),CB)
                mc=lax.broadcasted_iota(jnp.int32,(Q,CB),1)+j*CB>=c0
                xr=[];xi=[]
                for m in range(4):
                    mr=lax.broadcasted_iota(jnp.int32,(Q,CB),0)+m*Q>=r
                    w=[]
                    for p in range(2):
                        rt=slice(m*Q,(m+1)*Q); rl=slice(M+m*Q,M+(m+1)*Q)
                        v=jnp.where(mr,jnp.where(mc,X[p,rt,b1],X[p,rt,b2]),jnp.where(mc,X[p,rl,b1],X[p,rl,b2]))
                        W[p,rt,cols]=v; w.append(v)
                    pr=PR[0,rt,cols]; pi=PR[1,rt,cols]
                    xr.append(w[0]*pr-w[1]*pi); xi.append(w[0]*pi+w[1]*pr)
                for q,(yr,yi) in enumerate(fly_in(xr,xi)):
                    o=lmul(mh[q],ml[q],jnp.concatenate([yr,yi],axis=0))
                    H[0,q*Q:(q+1)*Q,cols]=o[:Q]; H[1,q*Q:(q+1)*Q,cols]=o[Q:]
            @pl.loop(0,M//RB)
            def _(j):
                rows=pl.ds(pl.multiple_of(j*RB,RB),RB)
                xr=[H[0,rows,m*Q:(m+1)*Q] for m in range(4)]; xi=[H[1,rows,m*Q:(m+1)*Q] for m in range(4)]
                e=[]
                for q,(yr,yi) in enumerate(fly_in(xr,xi)):
                    f=rmul(jnp.concatenate([yr,yi],axis=1),th[q],tl[q])
                    fr=f[:,:Q]; fi=f[:,Q:]
                    fac=1.0-AP[s,rows,q*Q:(q+1)*Q]*lax.rsqrt(fr*fr+fi*fi+1.0)
                    o=rmul(jnp.concatenate([fac*fr,fac*fi],axis=1),mh[q],ml[q])
                    e.append((o[:,:Q],o[:,Q:]))
                for m,(zr,zi) in enumerate(fly_out(e)):
                    H[0,rows,m*Q:(m+1)*Q]=zr; H[1,rows,m*Q:(m+1)*Q]=zi
            @pl.loop(0,M//CB)
            def _(j):
                cols=pl.ds(pl.multiple_of(j*CB,CB),CB)
                b1=pl.ds(pl.multiple_of(qc*M+j*CB,CB),CB); b2=pl.ds(pl.multiple_of(qc*M+M+j*CB,CB),CB)
                mc=lax.broadcasted_iota(jnp.int32,(Q,CB),1)+j*CB>=c0
                e=[]
                for q in range(4):
                    o=lmul(th[q],tl[q],jnp.concatenate([H[0,q*Q:(q+1)*Q,cols],H[1,q*Q:(q+1)*Q,cols]],axis=0))
                    e.append((o[:Q],o[Q:]))
                for m,(sr,si) in enumerate(fly_out(e)):
                    mr=lax.broadcasted_iota(jnp.int32,(Q,CB),0)+m*Q>=r
                    rt=slice(m*Q,(m+1)*Q); rl=slice(M+m*Q,M+(m+1)*Q)
                    pr=PR[0,rt,cols]; pi=PR[1,rt,cols]
                    wr=W[0,rt,cols]; wi=W[1,rt,cols]
                    g=(pr*sr+pi*si,pr*si-pi*sr); d=(wr*sr+wi*si,wr*si-wi*sr)
                    for p in range(2):
                        D[p,rt,cols]=d[p]; D[p,rl,cols]=d[p]
                        gt=jnp.where(mr,g[p],0.0); gl=g[p]-gt
                        g1=jnp.where(mc,gt,0.0); G[p,rt,b1]+=g1; G[p,rt,b2]+=gt-g1
                        g1=jnp.where(mc,gl,0.0); G[p,rl,b1]+=g1; G[p,rl,b2]+=gl-g1
            @pl.loop(0,4)
            def _(b):
                for p in range(2):
                    x=rows_from(D,p,r+b*Q)
                    DP[p,pl.ds(pl.multiple_of(b*Q,Q),Q),:]+=pltpu.roll(x,lax.rem(M-c0,M),1)
    o1=pltpu.make_async_copy(G,G_h,osem.at[0]); o2=pltpu.make_async_copy(DP,DP_h,osem.at[1])
    o1.start(); o2.start(); o1.wait(); o2.wait()

def compute(off,live,X,R,L,C,amp,pup):
    hi,lo,th,tl,pm=[jnp.asarray(t) for t in tables()]
    sm=pl.BlockSpec(memory_space=pltpu.SMEM); an=pl.BlockSpec(memory_space=pl.ANY); vm=pl.BlockSpec(memory_space=pltpu.VMEM)
    V=pltpu.VMEM
    return pl.pallas_call(kern2,
        out_shape=[jax.ShapeDtypeStruct((2,1024,1536),F32),jax.ShapeDtypeStruct((2,M,M),F32)],
        in_specs=[sm,sm]+[an]*6+[vm]*6, out_specs=[an,an],
        scratch_shapes=[V((2,1024,1536),F32),V((2,1024,1536),F32),V((3,M,M),F32),V((3,M,M),F32),V((2,2*M,M),F32),
            V((2,M,M),F32),V((2,M,M),F32),V((2,M,M),F32),V((2,2*M,M),F32),V((2,M,M),F32),
            pltpu.SemaphoreType.DMA((7,)),pltpu.SemaphoreType.DMA((2,))],
        compiler_params=pltpu.CompilerParams(vmem_limit_bytes=62*1024*1024),
        name="slots",
        cost_estimate=pl.CostEstimate(flops=3*4*3*2*512*512*256,bytes_accessed=31*2**20,transcendentals=3*512*512))(off,live,X,R,L,C,amp,pup,hi,lo,th,tl,pm,pm.T)


MESH = pl.DeviceIdType.MESH
LOW = pl.ds(0, 256)
HIGH = pl.ds(256, 256)
LEFT = pl.ds(0, 512)
RIGHT = pl.ds(512, 512)
WHOLE = pl.ds(0, 512)


def when(cond, run):
    pl.when(cond)(run)


def greet(partners):
    barrier = pltpu.get_barrier_semaphore()
    count = jnp.int32(0)
    for cond, device in partners:
        count = count + jnp.where(cond, 1, 0).astype(jnp.int32)

        @pl.when(cond)
        def _():
            pl.semaphore_signal(barrier, inc=1, device_id=device, device_id_type=MESH)

    pl.semaphore_wait(barrier, count)


class Place:
    def __init__(self):
        ty = lax.axis_index("ty")
        tx = lax.axis_index("tx")
        self.ty, self.tx = ty, tx
        self.has_u, self.has_d = ty > 0, ty < N_TY - 1
        self.has_l, self.has_r = tx > 0, tx < N_TX - 1
        self.odd = lax.rem(ty, 2) == 1
        self.even = lax.rem(ty, 2) == 0
        self.up, self.down = (ty - 1, tx), (ty + 1, tx)
        self.left, self.right = (ty, tx - 1), (ty, tx + 1)

    def neighbours(self):
        return [
            (self.has_u, self.up),
            (self.has_d, self.down),
            (self.has_l, self.left),
            (self.has_r, self.right),
        ]


def fetch_kernel(tile, strip_r, strip_l, strip_c, relay_l, relay_r, ss, rs):
    me = Place()
    ty, tx = me.ty, me.tx
    yh, xh = N_TY // 2, N_TX // 2
    y_from, y_via, y_to = ty == yh, ty == N_TY - 1, ty == yh - 1
    x_from, x_via, x_to = tx == xh, tx == N_TX - 1, tx == xh - 1
    greet(
        me.neighbours()
        + [
            (y_from, (N_TY - 1, tx)),
            (y_via, (yh, tx)),
            (y_via, (yh - 1, tx)),
            (y_to, (N_TY - 1, tx)),
            (x_from, (ty, N_TX - 1)),
            (x_via, (ty, xh)),
            (x_via, (ty, xh - 1)),
            (x_to, (ty, N_TX - 1)),
        ]
    )

    def rc(k, src, dst, dev, rk=None):
        return pltpu.make_async_remote_copy(
            src_ref=src,
            dst_ref=dst,
            send_sem=ss.at[k],
            recv_sem=rs.at[k if rk is None else rk],
            device_id=dev,
            device_id_type=MESH,
        )

    ra = rc(0, tile.at[:, LOW, LEFT], strip_r.at[:, LOW, :], me.left)
    rb = rc(1, tile.at[:, HIGH, LEFT], strip_r.at[:, HIGH, :], me.left)
    rb_out = rc(1, tile.at[:, HIGH, LEFT], relay_r, (ty, N_TX - 1), 10)
    rb_fwd = rc(10, relay_r, strip_r.at[:, HIGH, :], (ty, xh - 1), 1)
    l0b = rc(2, tile.at[:, HIGH, LEFT], strip_l.at[:, HIGH, LEFT], me.up)
    l0a = rc(3, tile.at[:, LOW, LEFT], strip_l.at[:, LOW, LEFT], me.up)
    l1 = [
        rc(4, tile.at[:, LOW, RIGHT], strip_l.at[:, LOW, RIGHT], me.up),
        rc(5, tile.at[:, HIGH, RIGHT], strip_l.at[:, HIGH, RIGHT], me.up),
    ]
    l1_out = [
        rc(4, tile.at[:, LOW, RIGHT], relay_l.at[:, LOW, :], (N_TY - 1, tx), 8),
        rc(5, tile.at[:, HIGH, RIGHT], relay_l.at[:, HIGH, :], (N_TY - 1, tx), 9),
    ]
    l1_fwd = [
        rc(8, relay_l.at[:, LOW, :], strip_l.at[:, LOW, RIGHT], (yh - 1, tx), 4),
        rc(9, relay_l.at[:, HIGH, :], strip_l.at[:, HIGH, RIGHT], (yh - 1, tx), 5),
    ]
    ca = rc(6, strip_r.at[:, LOW, :], strip_c.at[:, LOW, :], me.up)
    cb = rc(7, strip_r.at[:, HIGH, :], strip_c.at[:, HIGH, :], me.up)
    cz = rc(7, strip_l.at[:, HIGH, LEFT], strip_c.at[:, HIGH, :], me.left)

    when(me.has_l, ra.start)
    when(me.has_u, l0b.start)
    when(me.has_l & (tx != xh), rb.start)
    when(x_from, rb_out.start)
    for direct, out in zip(l1, l1_out):
        when(me.has_u & (ty != yh), direct.start)
        when(y_from, out.start)
    when(me.has_u, l0a.start)

    when(me.has_r, ra.wait_recv)
    when(me.has_r & me.has_u, ca.start)
    when(me.has_d, l0b.wait_recv)
    when(me.has_d & me.has_l & me.odd, cz.start)

    def pass_rb():
        rb_out.wait_recv()
        rb_fwd.start()

    when(x_via, pass_rb)
    for out, fwd in zip(l1_out, l1_fwd):

        def pass_l1():
            out.wait_recv()
            fwd.start()

        when(y_via, pass_l1)
    when(me.has_r, rb.wait_recv)
    when(me.has_r & me.has_u & me.odd, cb.start)

    def rest():
        l0a.wait_recv()
        l1[0].wait_recv()
        l1[1].wait_recv()

    when(me.has_d, rest)
    when(me.has_d & me.has_r, ca.wait_recv)
    when(me.has_d & me.has_r, cz.wait_recv)
    when(me.has_l, ra.wait_send)
    when(me.has_l, rb.wait_send)

    def sent_l():
        l0b.wait_send()
        l0a.wait_send()
        l1[0].wait_send()
        l1[1].wait_send()

    when(me.has_u, sent_l)
    when(me.has_r & me.has_u, ca.wait_send)
    when(me.has_r & me.has_u & me.odd, cb.wait_send)
    when(me.has_d & me.has_l & me.odd, cz.wait_send)
    when(x_via, rb_fwd.wait_send)

    def sent_fwd():
        l1_fwd[0].wait_send()
        l1_fwd[1].wait_send()

    when(y_via, sent_fwd)


def fetch(tile):
    return pl.pallas_call(
        fetch_kernel,
        out_shape=[
            jax.ShapeDtypeStruct((2, M, M), F32),
            jax.ShapeDtypeStruct((2, M, 2 * M), F32),
            jax.ShapeDtypeStruct((2, M, M), F32),
        ],
        in_specs=[pl.BlockSpec(memory_space=pl.ANY)],
        out_specs=[pl.BlockSpec(memory_space=pl.ANY)] * 3,
        scratch_shapes=[
            pltpu.VMEM((2, M, M), F32),
            pltpu.VMEM((2, M // 2, M), F32),
            pltpu.SemaphoreType.DMA((11,)),
            pltpu.SemaphoreType.DMA((11,)),
        ],
        name="fetch_strips",
        compiler_params=pltpu.CompilerParams(collective_id=0, has_side_effects=True),
    )(tile)


def give_kernel(
    grads, dpup, out, pup, own, g_r, g_l, got_l, got_r, got_c, got_z, relay_l, relay_r, part, sums, rows_a, rows_b, rows_c, ls, ss, rs, ps, pr
):
    me = Place()
    ty, tx = me.ty, me.tx
    yh, xh = N_TY // 2, N_TX // 2
    y_from, y_via, y_to = ty == yh - 1, ty == 0, ty == yh
    x_from, x_via, x_to = tx == xh - 1, tx == 0, tx == xh
    core = lax.rem(ty, 2)
    x = (ty // 8) * 2 + tx // 4
    y = lax.rem(ty, 8) // 2
    z = lax.rem(tx, 4)

    def device(px, py, pz):
        return ((px // 2) * 8 + py * 2 + core, lax.rem(px, 2) * 4 + pz)

    mate = (ty + 1 - 2 * core, tx)
    peers_x = [device(lax.rem(x + d, 4), y, z) for d in (1, 2, 3)]
    peers_y = [device(x, lax.rem(y + d, 4), z) for d in (1, 2, 3)]
    peers_z = [device(x, y, lax.rem(z + d, 4)) for d in (1, 2, 3)]
    always = ty >= 0
    greet(
        me.neighbours()
        + [
            (y_from, (0, tx)),
            (y_via, (yh - 1, tx)),
            (y_via, (yh, tx)),
            (y_to, (0, tx)),
            (x_from, (ty, 0)),
            (x_via, (ty, xh - 1)),
            (x_via, (ty, xh)),
            (x_to, (ty, 0)),
        ]
        + [(always, d) for d in [mate] + peers_x + peers_y + peers_z]
    )

    def rc(k, src, dst, dev, rk=None):
        return pltpu.make_async_remote_copy(
            src_ref=src,
            dst_ref=dst,
            send_sem=ss.at[k],
            recv_sem=rs.at[k if rk is None else rk],
            device_id=dev,
            device_id_type=MESH,
        )

    def pc(k, src, dst, dev):
        return pltpu.make_async_remote_copy(
            src_ref=src,
            dst_ref=dst,
            send_sem=ps.at[k],
            recv_sem=pr.at[k],
            device_id=dev,
            device_id_type=MESH,
        )

    top = pl.ds(M, 256)
    bottom = pl.ds(M + 256, 256)
    far = pl.ds(2 * M, M)
    load_p = pltpu.make_async_copy(dpup.at[core], part, ls.at[0])
    load_r = pltpu.make_async_copy(grads.at[:, WHOLE, far], g_r, ls.at[1])
    load_l = pltpu.make_async_copy(grads.at[:, bottom, LEFT], g_l, ls.at[2])
    load_o = pltpu.make_async_copy(grads.at[:, WHOLE, pl.ds(0, 2 * M)], own, ls.at[3])

    pair = pc(0, dpup.at[1 - core], sums, mate)
    ca = rc(0, grads.at[:, top, far], got_c.at[:, LOW, :], me.down)
    cb = rc(1, grads.at[:, bottom, far], got_c.at[:, HIGH, :], me.down)
    cz = rc(1, grads.at[:, bottom, far], got_z, me.right, 2)
    l0a = rc(3, grads.at[:, top, LEFT], got_l.at[:, LOW, LEFT], me.down)
    l0b = rc(4, g_l, got_l.at[:, HIGH, LEFT], me.down)
    l1 = [
        rc(5, grads.at[:, top, RIGHT], got_l.at[:, LOW, RIGHT], me.down),
        rc(6, grads.at[:, bottom, RIGHT], got_l.at[:, HIGH, RIGHT], me.down),
    ]
    l1_out = [
        rc(5, grads.at[:, top, RIGHT], relay_l.at[:, LOW, :], (0, tx), 9),
        rc(6, grads.at[:, bottom, RIGHT], relay_l.at[:, HIGH, :], (0, tx), 10),
    ]
    l1_fwd = [
        rc(9, relay_l.at[:, LOW, :], got_l.at[:, LOW, RIGHT], (yh, tx), 5),
        rc(10, relay_l.at[:, HIGH, :], got_l.at[:, HIGH, RIGHT], (yh, tx), 6),
    ]
    ra = rc(7, g_r.at[:, LOW, :], got_r.at[:, LOW, :], me.right)
    rb = rc(8, g_r.at[:, HIGH, :], got_r.at[:, HIGH, :], me.right)
    ra_out = rc(7, g_r.at[:, LOW, :], relay_r, (ty, 0), 11)
    ra_fwd = rc(11, relay_r, got_r.at[:, LOW, :], (ty, xh), 7)

    load_p.start()
    load_r.start()
    load_l.start()
    pair.start()
    has_c = me.has_d & me.has_r
    when(has_c, ca.start)
    when(has_c & me.even, cb.start)
    when(has_c & me.odd, cz.start)
    for direct, out_l in zip(l1, l1_out):
        when(me.has_d & (ty != yh - 1), direct.start)
        when(y_from, out_l.start)
    when(me.has_d, l0a.start)
    load_o.start()

    load_r.wait()
    load_l.wait()
    when(me.has_r & me.even, rb.start)
    when(me.has_d & (me.even | (tx == 0)), l0b.start)

    load_p.wait()
    pair.wait_recv()
    sums[...] += part[...]

    quarter = M // 4

    def share(base, step, peers, src, dst, rows, mine):
        copies = []
        for d in range(3):
            to = lax.rem(mine + d + 1, 4)
            copies.append(
                pc(base + d, src.at[pl.ds(pl.multiple_of(to * rows, rows), rows), :], dst.at[d], peers[d])
            )
        for copy in copies:
            copy.start()
        return copies

    def own_rows(src, rows, mine):
        return src[pl.ds(pl.multiple_of(mine * rows, rows), rows), :]

    sent = share(1, 0, peers_x, sums, rows_a, 128, x)

    def add_c_low():
        ca.wait_recv()
        g_r[:, LOW, :] += got_c[:, LOW, :]

    when(me.has_u & me.has_r, add_c_low)
    when(me.has_r & (tx != xh - 1), ra.start)
    when(x_from, ra_out.start)

    def add_c_high():
        cb.wait_recv()
        g_r[:, HIGH, :] += got_c[:, HIGH, :]
        rb.start()

    when(me.has_r & me.odd, add_c_high)

    def add_z():
        cz.wait_recv()
        g_l[...] += got_z[...]
        l0b.start()

    when(me.has_d & me.odd & (tx > 0), add_z)

    for copy in sent:
        copy.wait_recv()
    part[0:128, :] = own_rows(sums, 128, x) + rows_a[0] + rows_a[1] + rows_a[2]
    sent_y = share(4, 1, peers_y, part, rows_b, 32, y)

    def pass_ra():
        ra_out.wait_recv()
        ra_fwd.start()

    when(x_via, pass_ra)
    for out_l, fwd in zip(l1_out, l1_fwd):

        def pass_l1():
            out_l.wait_recv()
            fwd.start()

        when(y_via, pass_l1)

    for copy in sent_y:
        copy.wait_recv()
    part[128:160, :] = own_rows(part, 32, y) + rows_b[0] + rows_b[1] + rows_b[2]
    sent_z = share(7, 2, peers_z, part.at[pl.ds(128, 32)], rows_c, 8, z)
    for copy in sent_z:
        copy.wait_recv()
    norm = 1.0 / math.sqrt(N_TY * N_TX)
    base = x * 128 + y * 32 + z * 8
    total = own_rows(part.at[pl.ds(128, 32)], 8, z) + rows_c[0] + rows_c[1] + rows_c[2]
    pup[core, pl.ds(pl.multiple_of(base, 8), 8), :] = total * norm

    def spread(base_k, start, rows, peers):
        here = pup.at[core, pl.ds(pl.multiple_of(start, rows), rows), :]
        copies = [pc(base_k + d, here, here, peers[d]) for d in range(3)]
        for copy in copies:
            copy.start()
        for copy in copies:
            copy.wait_recv()
        return copies

    all_sent = sent + sent_y + sent_z
    all_sent += spread(10, base, 8, peers_z)
    all_sent += spread(13, x * 128 + y * 32, 32, peers_y)
    all_sent += spread(16, x * 128, 128, peers_x)
    last = pc(19, pup.at[core], pup.at[core], mate)
    last.start()

    load_o.wait()

    def add_l():
        l0a.wait_recv()
        l0b.wait_recv()
        l1[0].wait_recv()
        l1[1].wait_recv()

    when(me.has_u, add_l)

    def add_r():
        ra.wait_recv()
        rb.wait_recv()

    when(me.has_l, add_r)

    @pl.loop(0, 16)
    def _(i):
        rows = pl.ds(pl.multiple_of(i * 32, 32), 32)
        out[:, rows, :] = own[:, rows, :]

        @pl.when(me.has_u)
        def _():
            out[:, rows, :] += got_l[:, rows, :]

        @pl.when(me.has_l)
        def _():
            out[:, rows, 0:M] += got_r[:, rows, :]

    last.wait_recv()
    pair.wait_send()
    last.wait_send()
    for copy in all_sent:
        copy.wait_send()
    when(has_c, ca.wait_send)
    when(has_c, cb.wait_send)

    def sent_l():
        l0a.wait_send()
        l0b.wait_send()
        l1[0].wait_send()
        l1[1].wait_send()

    when(me.has_d, sent_l)

    def sent_r():
        ra.wait_send()
        rb.wait_send()

    when(me.has_r, sent_r)
    when(x_via, ra_fwd.wait_send)

    def sent_fwd():
        l1_fwd[0].wait_send()
        l1_fwd[1].wait_send()

    when(y_via, sent_fwd)


def give(grads, dpup):
    vmem = pltpu.VMEM
    return pl.pallas_call(
        give_kernel,
        out_shape=[
            jax.ShapeDtypeStruct((2, M, 2 * M), F32),
            jax.ShapeDtypeStruct((2, M, M), F32),
        ],
        in_specs=[pl.BlockSpec(memory_space=pl.ANY)] * 2,
        out_specs=[pl.BlockSpec(memory_space=pltpu.VMEM)] * 2,
        scratch_shapes=[
            vmem((2, M, 2 * M), F32),
            vmem((2, M, M), F32),
            vmem((2, M // 2, M), F32),
            vmem((2, M, 2 * M), F32),
            vmem((2, M, M), F32),
            vmem((2, M, M), F32),
            vmem((2, M // 2, M), F32),
            vmem((2, M, M), F32),
            vmem((2, M // 2, M), F32),
            vmem((M, M), F32),
            vmem((M, M), F32),
            vmem((3, 128, M), F32),
            vmem((3, 32, M), F32),
            vmem((3, 8, M), F32),
            pltpu.SemaphoreType.DMA((4,)),
            pltpu.SemaphoreType.DMA((12,)),
            pltpu.SemaphoreType.DMA((12,)),
            pltpu.SemaphoreType.DMA((20,)),
            pltpu.SemaphoreType.DMA((20,)),
        ],
        name="give_back",
        compiler_params=pltpu.CompilerParams(
            collective_id=1, has_side_effects=True, vmem_limit_bytes=60 * 1024 * 1024
        ),
    )(grads, dpup)


def body(spectrum, pupil, amplitudes, offsets, live):
    strip_r, strip_l, strip_c = fetch(spectrum)
    grads, dpup = compute(offsets, live, spectrum, strip_r, strip_l, strip_c, amplitudes, pupil)
    return tuple(give(grads, dpup))


def solution(mesh):
    return jax.shard_map(
        body,
        mesh=mesh,
        in_specs=(
            P(None, "ty", "tx"),
            P(),
            P(("ty", "tx"), None, None),
            P(("ty", "tx"), None),
            P(("ty", "tx")),
        ),
        out_specs=(P(None, "ty", "tx"), P()),
        check_vma=False,
    )
```

time: 699 us -> 219 us (0.31)
  the two profiles are of different devices: /device:TPU:1 before, /device:TPU:125 now
where the time goes in v1:
time: 219 us; the launch traced here: 215 us
  Pallas kernels  207 us (95%)
  local copies, waits for them, and re-layouts  7.6 us (3%)
    pallas_call x1, Pallas kernels, give(): pl.pallas_call(give_kernel, out_shape=[jax.ShapeDtypeStruct((2, M, 2 * M)...  131 us
    pallas_call x1, Pallas kernels, fetch(): pl.pallas_call(fetch_kernel, out_shape=[jax.ShapeDtypeStruct((2, M, M), F...  51.4 us
    pallas_call x1, Pallas kernels, compute(): pl.pallas_call(kern2, out_shape=[jax.ShapeDtypeStruct((2, 1024, 1536), F3...  24.5 us
    unnamed x5, local copies, waits for them, and re-layouts  7.6 us

profile of v1, /device:TPU:125, one launch (start us, length us, event | category | flops | bytes accessed | tf_op | source)
XLA Modules:
  0.0 215.0 jit_solution(14675160302682766542)
XLA Ops:
  0.6 1.3 copy.12.off
  2.0 51.4 %fetch_strips.1 = (f32[2,512,512]{2,1,0:T(8,128)}, f32[2,512,1024]{2,1,0:T(8,128)}, f32[2,512,512]{2,1,0:T(8,128)}) custom-call(f32[2,512,1024]{2,1,0:T(8,128)} %X_h.1), custom_call_target="tpu_custom_call" | custom-call | tf_op jit(solution)/shard_map/fetch_strips/pallas_call | solution.py:330
  53.4 24.5 %slots.1 = (f32[2,1024,1536]{2,1,0:T(8,128)}, f32[2,512,512]{2,1,0:T(8,128)}) custom-call(s32[3,2]{1,0:T(4,128)} %copy.12.off, s32[3]{0:T(128)} %live.1, f32[2,512,1024]{2,1,0:T(8,128)} %X_h.1, f32[2,512,512]{2,1,0:T(8,128)} %get-tuple-element.7.R_h, f32[2,512,1024]{2,1,0:T(8,128)} %get-tuple-element.8.L_h, f32[2,512,512]{2,1,0:T(8,128)} %get-tuple-element.9.C_h, ...), custom_call_target="tpu_custom_call" | custom-call | flops 4831838208 | bytes 32505856 | tf_op jit(solution)/shard_map/slots/pallas_call | solution.py:161
  77.8 130.9 %give_back.1 = (f32[2,512,1024]{2,1,0:T(8,128)}, f32[2,512,512]{2,1,0:T(8,128)}) custom-call(f32[2,1024,1536]{2,1,0:T(8,128)} %get-tuple-element.10.grads, f32[2,512,512]{2,1,0:T(8,128)} %get-tuple-element.11.dpup), custom_call_target="tpu_custom_call" | custom-call | tf_op jit(solution)/shard_map/give_back/pallas_call | solution.py:606
  208.8 0.0 copy-start
  208.8 4.9 %copy.15 = f32[2,512,1024]{2,1,0:T(8,128)} copy(f32[2,512,1024]{2,1,0:T(8,128)} %get-tuple-element.14) | data formatting | bytes 8388608
  213.7 0.0 copy-done
  213.7 1.3 copy.16
Async XLA Ops:
  208.8 4.9 %copy-start = (f32[2,512,512]{2,1,0:T(8,128)S(1)}, f32[2,512,512]{2,1,0:T(8,128)}, u32[]{:S(2)}) copy-start(f32[2,512,512]{2,1,0:T(8,128)} %get-tuple-element.15) | copy-start | bytes 6291460

commit v2 on v1

--- a/solution.py
+++ b/solution.py
@@ -53,120 +53,23 @@
     c=(e[1][0]+e[3][0],e[1][1]+e[3][1]); d=(e[1][0]-e[3][0],e[1][1]-e[3][1])
     return [(a[0]+c[0],a[1]+c[1]),(b[0]+d[1],b[1]-d[0]),(a[0]-c[0],a[1]-c[1]),(b[0]-d[1],b[1]+d[0])]
 
-CB=256; RB=256
-
-def rows_from(ref,p,start):
-    low=lax.rem(start,8)
-    x=ref[p,pl.ds(pl.multiple_of(start-low,8),Q+8),:]
-    return pltpu.roll(x,lax.rem(Q+8-low,Q+8),0)[:Q]
-
-def kern2(off, live, X_h, R_h, L_h, C_h, amp_h, pup_h, mh, ml, th, tl, pm, pt, G_h, DP_h,
-          X, G, A, AP, PP, PR, W, H, D, DP, sem, osem):
-    cps=[]
-    for i,(s,d) in enumerate([(pup_h,PP.at[:,0:M]),(pup_h,PP.at[:,M:2*M]),(amp_h,A),
-                 (X_h,X.at[:,0:M,0:1024]),(R_h,X.at[:,0:M,1024:1536]),
-                 (L_h,X.at[:,M:2*M,0:1024]),(C_h,X.at[:,M:2*M,1024:1536])]):
-        cp=pltpu.make_async_copy(s,d,sem.at[i]); cp.start(); cps.append(cp)
-    r0=lax.axis_index("ty")*512; c0_=lax.axis_index("tx")*1024
-    @pl.loop(0,16)
-    def _(i):
-        G[:,pl.ds(pl.multiple_of(i*64,64),64),:]=jnp.zeros((2,64,1536),F32)
-    DP[...]=jnp.zeros((2,M,M),F32)
-    for cp in cps[0:3]: cp.wait()
-    @pl.loop(0,3)
-    def _(s):
-        @pl.when(live[s]>0)
-        def _():
-            for q in range(2):
-                h,l=split(A[s,q*RB:(q+1)*RB,:])
-                H[0,q*RB:(q+1)*RB,:]=dot(jnp.concatenate([h,l],axis=1),jnp.concatenate([pm[...],pm[...]],axis=0))
-            for q in range(2):
-                h,l=split(H[0,:,q*RB:(q+1)*RB])
-                AP[s,:,q*RB:(q+1)*RB]=dot(jnp.concatenate([pt[...],pt[...]],axis=1),jnp.concatenate([h,l],axis=0))
-    for cp in cps[3:]: cp.wait()
-    @pl.loop(0,3)
-    def _(s):
-        @pl.when(live[s]>0)
-        def _():
-            r=off[s,0]-r0; c=off[s,1]-c0_
-            qc=c//M; c0=c-qc*M
-            @pl.loop(0,4)
-            def _(b):
-                for p in range(2):
-                    x=rows_from(PP,p,lax.rem(M-r,M)+b*Q)
-                    PR[p,pl.ds(pl.multiple_of(b*Q,Q),Q),:]=pltpu.roll(x,c0,1)
-            @pl.loop(0,M//CB)
-            def _(j):
-                cols=pl.ds(pl.multiple_of(j*CB,CB),CB)
-                b1=pl.ds(pl.multiple_of(qc*M+j*CB,CB),CB); b2=pl.ds(pl.multiple_of(qc*M+M+j*CB,CB),CB)
-                mc=lax.broadcasted_iota(jnp.int32,(Q,CB),1)+j*CB>=c0
-                xr=[];xi=[]
-                for m in range(4):
-                    mr=lax.broadcasted_iota(jnp.int32,(Q,CB),0)+m*Q>=r
-                    w=[]
-                    for p in range(2):
-                        rt=slice(m*Q,(m+1)*Q); rl=slice(M+m*Q,M+(m+1)*Q)
-                        v=jnp.where(mr,jnp.where(mc,X[p,rt,b1],X[p,rt,b2]),jnp.where(mc,X[p,rl,b1],X[p,rl,b2]))
-                        W[p,rt,cols]=v; w.append(v)
-                    pr=PR[0,rt,cols]; pi=PR[1,rt,cols]
-                    xr.append(w[0]*pr-w[1]*pi); xi.append(w[0]*pi+w[1]*pr)
-                for q,(yr,yi) in enumerate(fly_in(xr,xi)):
-                    o=lmul(mh[q],ml[q],jnp.concatenate([yr,yi],axis=0))
-                    H[0,q*Q:(q+1)*Q,cols]=o[:Q]; H[1,q*Q:(q+1)*Q,cols]=o[Q:]
-            @pl.loop(0,M//RB)
-            def _(j):
-                rows=pl.ds(pl.multiple_of(j*RB,RB),RB)
-                xr=[H[0,rows,m*Q:(m+1)*Q] for m in range(4)]; xi=[H[1,rows,m*Q:(m+1)*Q] for m in range(4)]
-                e=[]
-                for q,(yr,yi) in enumerate(fly_in(xr,xi)):
-                    f=rmul(jnp.concatenate([yr,yi],axis=1),th[q],tl[q])
-                    fr=f[:,:Q]; fi=f[:,Q:]
-                    fac=1.0-AP[s,rows,q*Q:(q+1)*Q]*lax.rsqrt(fr*fr+fi*fi+1.0)
-                    o=rmul(jnp.concatenate([fac*fr,fac*fi],axis=1),mh[q],ml[q])
-                    e.append((o[:,:Q],o[:,Q:]))
-                for m,(zr,zi) in enumerate(fly_out(e)):
-                    H[0,rows,m*Q:(m+1)*Q]=zr; H[1,rows,m*Q:(m+1)*Q]=zi
-            @pl.loop(0,M//CB)
-            def _(j):
-                cols=pl.ds(pl.multiple_of(j*CB,CB),CB)
-                b1=pl.ds(pl.multiple_of(qc*M+j*CB,CB),CB); b2=pl.ds(pl.multiple_of(qc*M+M+j*CB,CB),CB)
-                mc=lax.broadcasted_iota(jnp.int32,(Q,CB),1)+j*CB>=c0
-                e=[]
-                for q in range(4):
-                    o=lmul(th[q],tl[q],jnp.concatenate([H[0,q*Q:(q+1)*Q,cols],H[1,q*Q:(q+1)*Q,cols]],axis=0))
-                    e.append((o[:Q],o[Q:]))
-                for m,(sr,si) in enumerate(fly_out(e)):
-                    mr=lax.broadcasted_iota(jnp.int32,(Q,CB),0)+m*Q>=r
-                    rt=slice(m*Q,(m+1)*Q); rl=slice(M+m*Q,M+(m+1)*Q)
-                    pr=PR[0,rt,cols]; pi=PR[1,rt,cols]
-                    wr=W[0,rt,cols]; wi=W[1,rt,cols]
-                    g=(pr*sr+pi*si,pr*si-pi*sr); d=(wr*sr+wi*si,wr*si-wi*sr)
-                    for p in range(2):
-                        D[p,rt,cols]=d[p]; D[p,rl,cols]=d[p]
-                        gt=jnp.where(mr,g[p],0.0); gl=g[p]-gt
-                        g1=jnp.where(mc,gt,0.0); G[p,rt,b1]+=g1; G[p,rt,b2]+=gt-g1
-                        g1=jnp.where(mc,gl,0.0); G[p,rl,b1]+=g1; G[p,rl,b2]+=gl-g1
-            @pl.loop(0,4)
-            def _(b):
-                for p in range(2):
-                    x=rows_from(D,p,r+b*Q)
-                    DP[p,pl.ds(pl.multiple_of(b*Q,Q),Q),:]+=pltpu.roll(x,lax.rem(M-c0,M),1)
-    o1=pltpu.make_async_copy(G,G_h,osem.at[0]); o2=pltpu.make_async_copy(DP,DP_h,osem.at[1])
-    o1.start(); o2.start(); o1.wait(); o2.wait()
-
-def compute(off,live,X,R,L,C,amp,pup):
-    hi,lo,th,tl,pm=[jnp.asarray(t) for t in tables()]
-    sm=pl.BlockSpec(memory_space=pltpu.SMEM); an=pl.BlockSpec(memory_space=pl.ANY); vm=pl.BlockSpec(memory_space=pltpu.VMEM)
-    V=pltpu.VMEM
-    return pl.pallas_call(kern2,
-        out_shape=[jax.ShapeDtypeStruct((2,1024,1536),F32),jax.ShapeDtypeStruct((2,M,M),F32)],
-        in_specs=[sm,sm]+[an]*6+[vm]*6, out_specs=[an,an],
-        scratch_shapes=[V((2,1024,1536),F32),V((2,1024,1536),F32),V((3,M,M),F32),V((3,M,M),F32),V((2,2*M,M),F32),
-            V((2,M,M),F32),V((2,M,M),F32),V((2,M,M),F32),V((2,2*M,M),F32),V((2,M,M),F32),
-            pltpu.SemaphoreType.DMA((7,)),pltpu.SemaphoreType.DMA((2,))],
-        compiler_params=pltpu.CompilerParams(vmem_limit_bytes=62*1024*1024),
-        name="slots",
-        cost_estimate=pl.CostEstimate(flops=3*4*3*2*512*512*256,bytes_accessed=31*2**20,transcendentals=3*512*512))(off,live,X,R,L,C,amp,pup,hi,lo,th,tl,pm,pm.T)
+
+def permute(load, mid, store, left, right):
+    for q in range(2):
+        part = slice(q * 256, (q + 1) * 256)
+        h, l = split(load(part))
+        mid[part, :] = dot(jnp.concatenate([h, l], axis=1), jnp.concatenate([right, right], axis=0))
+    for q in range(2):
+        part = slice(q * 256, (q + 1) * 256)
+        h, l = split(mid[:, part])
+        store(part, dot(jnp.concatenate([left, left], axis=1), jnp.concatenate([h, l], axis=0)))
+
+
+def shifted(by, axis):
+    a = lax.broadcasted_iota(jnp.int32, (M, M), axis)
+    b = lax.broadcasted_iota(jnp.int32, (M, M), 1 - axis) + by
+    b = jnp.where(b >= M, b - M, b)
+    return jnp.where(a == b, 1.0, 0.0).astype(BF)
 
 
 MESH = pl.DeviceIdType.MESH
@@ -215,7 +118,13 @@
         ]
 
 
-def fetch_kernel(tile, strip_r, strip_l, strip_c, relay_l, relay_r, ss, rs):
+def slots_kernel(
+    off, live, tile, amp, pup, mh, ml, th, tl, pm, pt, grads, dpup,
+    X, G, A, AP, PP, PR, W, H, D, DP, relay_l, relay_a, relay_r, ls, ss, rs
+):
+    strip_r = X.at[:, 0:M, 2 * M : 3 * M]
+    strip_l = X.at[:, M : 2 * M, 0 : 2 * M]
+    strip_c = X.at[:, M : 2 * M, 2 * M : 3 * M]
     me = Place()
     ty, tx = me.ty, me.tx
     yh, xh = N_TY // 2, N_TX // 2
@@ -254,14 +163,17 @@
     l1 = [
         rc(4, tile.at[:, LOW, RIGHT], strip_l.at[:, LOW, RIGHT], me.up),
         rc(5, tile.at[:, HIGH, RIGHT], strip_l.at[:, HIGH, RIGHT], me.up),
+        l0a,
     ]
     l1_out = [
         rc(4, tile.at[:, LOW, RIGHT], relay_l.at[:, LOW, :], (N_TY - 1, tx), 8),
         rc(5, tile.at[:, HIGH, RIGHT], relay_l.at[:, HIGH, :], (N_TY - 1, tx), 9),
+        rc(3, tile.at[:, LOW, LEFT], relay_a, (N_TY - 1, tx), 11),
     ]
     l1_fwd = [
         rc(8, relay_l.at[:, LOW, :], strip_l.at[:, LOW, RIGHT], (yh - 1, tx), 4),
         rc(9, relay_l.at[:, HIGH, :], strip_l.at[:, HIGH, RIGHT], (yh - 1, tx), 5),
+        rc(11, relay_a, strip_l.at[:, LOW, LEFT], (yh - 1, tx), 3),
     ]
     ca = rc(6, strip_r.at[:, LOW, :], strip_c.at[:, LOW, :], me.up)
     cb = rc(7, strip_r.at[:, HIGH, :], strip_c.at[:, HIGH, :], me.up)
@@ -271,10 +183,50 @@
     when(me.has_u, l0b.start)
     when(me.has_l & (tx != xh), rb.start)
     when(x_from, rb_out.start)
-    for direct, out in zip(l1, l1_out):
-        when(me.has_u & (ty != yh), direct.start)
-        when(y_from, out.start)
-    when(me.has_u, l0a.start)
+    inner = tx < N_TX - 1
+    for i, (direct, out) in enumerate(zip(l1, l1_out)):
+        detour = y_from if i == 0 else y_from & inner
+        when(me.has_u & jnp.logical_not(detour), direct.start)
+        when(detour, out.start)
+
+    load_p = pltpu.make_async_copy(pup, PP.at[:, 0:M], ls.at[0])
+    load_a = pltpu.make_async_copy(amp, A, ls.at[1])
+    load_x = pltpu.make_async_copy(tile, X.at[:, 0:M, 0 : 2 * M], ls.at[2])
+    load_p.start()
+    load_a.start()
+    load_x.start()
+    row0 = ty * M
+    col0 = tx * 2 * M
+
+    @pl.loop(0, 16)
+    def _(i):
+        G[:, pl.ds(pl.multiple_of(i * 64, 64), 64), :] = jnp.zeros((2, 64, 3 * M), F32)
+
+    DP[...] = jnp.zeros((2, M, M), F32)
+    load_p.wait()
+
+    @pl.loop(0, 3)
+    def _(s):
+        r = off[s, 0] - row0
+        c0 = lax.rem(off[s, 1], M)
+
+        left = shifted(r, 0)
+        right = shifted(c0, 1)
+        for p in range(2):
+
+            def put(part, value):
+                PR[s, p, :, part] = value
+
+            permute(lambda part: PP[p, part, :], H.at[0], put, left, right)
+
+    load_a.wait()
+
+    @pl.loop(0, 3)
+    def _(s):
+        def put(part, value):
+            AP[s, :, part] = value
+
+        permute(lambda part: A[s, part, :], H.at[0], put, pt[...], pm[...])
 
     when(me.has_r, ra.wait_recv)
     when(me.has_r & me.has_u, ca.start)
@@ -286,13 +238,13 @@
         rb_fwd.start()
 
     when(x_via, pass_rb)
-    for out, fwd in zip(l1_out, l1_fwd):
+    for i, (out, fwd) in enumerate(zip(l1_out, l1_fwd)):
 
         def pass_l1():
             out.wait_recv()
             fwd.start()
 
-        when(y_via, pass_l1)
+        when(y_via if i == 0 else y_via & inner, pass_l1)
     when(me.has_r, rb.wait_recv)
     when(me.has_r & me.has_u & me.odd, cb.start)
 
@@ -319,32 +271,150 @@
     when(me.has_d & me.has_l & me.odd, cz.wait_send)
     when(x_via, rb_fwd.wait_send)
 
-    def sent_fwd():
-        l1_fwd[0].wait_send()
-        l1_fwd[1].wait_send()
-
-    when(y_via, sent_fwd)
-
-
-def fetch(tile):
+    for i, fwd in enumerate(l1_fwd):
+        when(y_via if i == 0 else y_via & inner, fwd.wait_send)
+
+    load_x.wait()
+    CB, RB = 256, 512
+
+    @pl.loop(0, 3)
+    def _(s):
+        r = off[s, 0] - row0
+        c = off[s, 1] - col0
+        qc = c // M
+        c0 = c - qc * M
+        weight = live[s].astype(F32)
+
+        @pl.loop(0, M // CB)
+        def _(j):
+            cols = pl.ds(pl.multiple_of(j * CB, CB), CB)
+            there = [pl.ds(pl.multiple_of(b * M + j * CB, CB), CB) for b in range(3)]
+            mc = lax.broadcasted_iota(jnp.int32, (Q, CB), 1) + j * CB >= c0
+            blk = jnp.where(mc, qc, qc + 1)
+            first, second = blk == 0, blk == 1
+            xr, xi = [], []
+            for m in range(4):
+                mr = lax.broadcasted_iota(jnp.int32, (Q, CB), 0) + m * Q >= r
+                rt = slice(m * Q, (m + 1) * Q)
+                rl = slice(M + m * Q, M + (m + 1) * Q)
+                w = []
+                for p in range(2):
+                    high = [X[p, rt, t] for t in there]
+                    low = [X[p, rl, t] for t in there]
+                    v = jnp.where(
+                        mr,
+                        jnp.where(first, high[0], jnp.where(second, high[1], high[2])),
+                        jnp.where(first, low[0], jnp.where(second, low[1], low[2])),
+                    )
+                    W[p, rt, cols] = v
+                    w.append(v)
+                pr = PR[s, 0, rt, cols]
+                pi = PR[s, 1, rt, cols]
+                xr.append(w[0] * pr - w[1] * pi)
+                xi.append(w[0] * pi + w[1] * pr)
+            for q, (yr, yi) in enumerate(fly_in(xr, xi)):
+                o = lmul(mh[q], ml[q], jnp.concatenate([yr, yi], axis=0))
+                H[0, q * Q : (q + 1) * Q, cols] = o[:Q]
+                H[1, q * Q : (q + 1) * Q, cols] = o[Q:]
+
+        for j in range(M // RB):
+            rows = slice(j * RB, (j + 1) * RB)
+            xr = [H[0, rows, m * Q : (m + 1) * Q] for m in range(4)]
+            xi = [H[1, rows, m * Q : (m + 1) * Q] for m in range(4)]
+            e = []
+            for q, (yr, yi) in enumerate(fly_in(xr, xi)):
+                f = rmul(jnp.concatenate([yr, yi], axis=1), th[q], tl[q])
+                fr, fi = f[:, :Q], f[:, Q:]
+                fac = 1.0 - AP[s, rows, q * Q : (q + 1) * Q] * lax.rsqrt(fr * fr + fi * fi + 1.0)
+                o = rmul(jnp.concatenate([fac * fr, fac * fi], axis=1), mh[q], ml[q])
+                e.append((o[:, :Q], o[:, Q:]))
+            for m, (zr, zi) in enumerate(fly_out(e)):
+                H[0, rows, m * Q : (m + 1) * Q] = zr
+                H[1, rows, m * Q : (m + 1) * Q] = zi
+
+        @pl.loop(0, M // CB)
+        def _(j):
+            cols = pl.ds(pl.multiple_of(j * CB, CB), CB)
+            mc = lax.broadcasted_iota(jnp.int32, (Q, CB), 1) + j * CB >= c0
+            blk = jnp.where(mc, qc, qc + 1)
+            e = []
+            for q in range(4):
+                z = jnp.concatenate([H[0, q * Q : (q + 1) * Q, cols], H[1, q * Q : (q + 1) * Q, cols]], axis=0)
+                o = lmul(th[q], tl[q], z)
+                e.append((o[:Q], o[Q:]))
+            for m, (sr, si) in enumerate(fly_out(e)):
+                mr = lax.broadcasted_iota(jnp.int32, (Q, CB), 0) + m * Q >= r
+                rt = slice(m * Q, (m + 1) * Q)
+                rl = slice(M + m * Q, M + (m + 1) * Q)
+                sr = sr * weight
+                si = si * weight
+                pr, pi = PR[s, 0, rt, cols], PR[s, 1, rt, cols]
+                wr, wi = W[0, rt, cols], W[1, rt, cols]
+                g = (pr * sr + pi * si, pr * si - pi * sr)
+                d = (wr * sr + wi * si, wr * si - wi * sr)
+                for p in range(2):
+                    D[p, rt, cols] = d[p]
+                    gt = jnp.where(mr, g[p], 0.0)
+                    gl = g[p] - gt
+                    for b in range(3):
+                        there = pl.ds(pl.multiple_of(b * M + j * CB, CB), CB)
+                        G[p, rt, there] += jnp.where(blk == b, gt, 0.0)
+                        G[p, rl, there] += jnp.where(blk == b, gl, 0.0)
+
+        left = shifted(r, 1)
+        right = shifted(c0, 0)
+        for p in range(2):
+
+            def put(part, value):
+                DP[p, :, part] += value
+
+            permute(lambda part: D[p, part, :], H.at[0], put, left, right)
+
+    out_g = pltpu.make_async_copy(G, grads, ls.at[0])
+    out_d = pltpu.make_async_copy(DP, dpup, ls.at[1])
+    out_g.start()
+    out_d.start()
+    out_g.wait()
+    out_d.wait()
+
+
+def slots(off, live, tile, amp, pup):
+    hi, lo, th, tl, pm = [jnp.asarray(t) for t in tables()]
+    smem = pl.BlockSpec(memory_space=pltpu.SMEM)
+    hbm = pl.BlockSpec(memory_space=pl.ANY)
+    vmem = pl.BlockSpec(memory_space=pltpu.VMEM)
+    V = pltpu.VMEM
     return pl.pallas_call(
-        fetch_kernel,
+        slots_kernel,
         out_shape=[
-            jax.ShapeDtypeStruct((2, M, M), F32),
-            jax.ShapeDtypeStruct((2, M, 2 * M), F32),
+            jax.ShapeDtypeStruct((2, 2 * M, 3 * M), F32),
             jax.ShapeDtypeStruct((2, M, M), F32),
         ],
-        in_specs=[pl.BlockSpec(memory_space=pl.ANY)],
-        out_specs=[pl.BlockSpec(memory_space=pl.ANY)] * 3,
+        in_specs=[smem, smem, hbm, hbm, hbm] + [vmem] * 6,
+        out_specs=[hbm, hbm],
         scratch_shapes=[
-            pltpu.VMEM((2, M, M), F32),
-            pltpu.VMEM((2, M // 2, M), F32),
-            pltpu.SemaphoreType.DMA((11,)),
-            pltpu.SemaphoreType.DMA((11,)),
+            V((2, 2 * M, 3 * M), F32),
+            V((2, 2 * M, 3 * M), F32),
+            V((3, M, M), F32),
+            V((3, M, M), F32),
+            V((2, M, M), F32),
+            V((3, 2, M, M), F32),
+            V((2, M, M), F32),
+            V((2, M, M), F32),
+            V((2, M, M), F32),
+            V((2, M, M), F32),
+            V((2, M, M), F32),
+            V((2, M // 2, M), F32),
+            V((2, M // 2, M), F32),
+            pltpu.SemaphoreType.DMA((3,)),
+            pltpu.SemaphoreType.DMA((12,)),
+            pltpu.SemaphoreType.DMA((12,)),
         ],
-        name="fetch_strips",
-        compiler_params=pltpu.CompilerParams(collective_id=0, has_side_effects=True),
-    )(tile)
+        name="fetch_and_slots",
+        compiler_params=pltpu.CompilerParams(
+            collective_id=0, has_side_effects=True, vmem_limit_bytes=63 * 1024 * 1024
+        ),
+    )(off, live, tile, amp, pup, hi, lo, th, tl, pm, pm.T)
 
 
 def give_kernel(
@@ -640,8 +710,7 @@
 
 
 def body(spectrum, pupil, amplitudes, offsets, live):
-    strip_r, strip_l, strip_c = fetch(spectrum)
-    grads, dpup = compute(offsets, live, spectrum, strip_r, strip_l, strip_c, amplitudes, pupil)
+    grads, dpup = slots(offsets, live, spectrum, amplitudes, pupil)
     return tuple(give(grads, dpup))
 
 

time: 219 us -> 211 us (0.963); the launches traced: 215 us -> 210 us
  Pallas kernels: 207 us -> 202 us
    pallas_call x1, Pallas kernels: 131 us -> 102 us  [give(): pl.pallas_call(give_kernel, out_shape=[jax.ShapeDtypeStruct((2, M, 2 * M)...]
    pallas_call x2 -> x1, Pallas kernels: 75.9 us -> 100 us  [slots(): pl.pallas_call(slots_kernel, out_shape=[jax.ShapeDtypeStruct((2, 2 * M, 3...]
where the time goes in v2:
time: 211 us; the launch traced here: 210 us
  Pallas kernels  202 us (96%)
  local copies, waits for them, and re-layouts  7.6 us (4%)
    pallas_call x1, Pallas kernels, give(): pl.pallas_call(give_kernel, out_shape=[jax.ShapeDtypeStruct((2, M, 2 * M)...  102 us
    pallas_call x1, Pallas kernels, slots(): pl.pallas_call(slots_kernel, out_shape=[jax.ShapeDtypeStruct((2, 2 * M, 3...  100 us
    unnamed x5, local copies, waits for them, and re-layouts  7.6 us

profile of v2, /device:TPU:125, one launch (start us, length us, event | category | flops | bytes accessed | tf_op | source)
XLA Modules:
  0.0 210.4 jit_solution(15215235036052838128)
XLA Ops:
  0.6 1.3 copy.12.off
  2.0 100.3 %fetch_and_slots.1 = (f32[2,1024,1536]{2,1,0:T(8,128)}, f32[2,512,512]{2,1,0:T(8,128)}) custom-call(s32[3,2]{1,0:T(4,128)} %copy.12.off, s32[3]{0:T(128)} %live.1, f32[2,512,1024]{2,1,0:T(8,128)} %tile.1, f32[3,512,512]{2,1,0:T(8,128)} %amp.1, f32[2,512,512]{2,1,0:T(8,128)} %pup.1, bf16[4,256,256]{2,1,0:T(8,128)(2,1)} %constant.10.clone.mh, ...), custom_call_target="tpu_custom_call" | custom-call | tf_op jit(solution)/shard_map/fetch_and_slots/pallas_call | solution.py:387
  102.2 101.9 %give_back.1 = (f32[2,512,1024]{2,1,0:T(8,128)}, f32[2,512,512]{2,1,0:T(8,128)}) custom-call(f32[2,1024,1536]{2,1,0:T(8,128)} %get-tuple-element.4.grads, f32[2,512,512]{2,1,0:T(8,128)} %get-tuple-element.5.dpup), custom_call_target="tpu_custom_call" | custom-call | tf_op jit(solution)/shard_map/give_back/pallas_call | solution.py:676
  204.1 0.0 copy-start
  204.1 4.9 %copy.15 = f32[2,512,1024]{2,1,0:T(8,128)} copy(f32[2,512,1024]{2,1,0:T(8,128)} %get-tuple-element.8) | data formatting | bytes 8388608
  209.1 0.0 copy-done
  209.1 1.3 copy.16
Async XLA Ops:
  204.1 4.9 %copy-start = (f32[2,512,512]{2,1,0:T(8,128)S(1)}, f32[2,512,512]{2,1,0:T(8,128)}, u32[]{:S(2)}) copy-start(f32[2,512,512]{2,1,0:T(8,128)} %get-tuple-element.9) | copy-start | bytes 6291460

commit v3 on v2

--- a/solution.py
+++ b/solution.py
@@ -501,8 +501,8 @@
     ]
     ra = rc(7, g_r.at[:, LOW, :], got_r.at[:, LOW, :], me.right)
     rb = rc(8, g_r.at[:, HIGH, :], got_r.at[:, HIGH, :], me.right)
-    ra_out = rc(7, g_r.at[:, LOW, :], relay_r, (ty, 0), 11)
-    ra_fwd = rc(11, relay_r, got_r.at[:, LOW, :], (ty, xh), 7)
+    rb_out = rc(8, g_r.at[:, HIGH, :], relay_r, (ty, 0), 11)
+    rb_fwd = rc(11, relay_r, got_r.at[:, HIGH, :], (ty, xh), 8)
 
     load_p.start()
     load_r.start()
@@ -520,7 +520,8 @@
 
     load_r.wait()
     load_l.wait()
-    when(me.has_r & me.even, rb.start)
+    when(me.has_r & me.even & (tx != xh - 1), rb.start)
+    when(x_from & me.even, rb_out.start)
     when(me.has_d & (me.even | (tx == 0)), l0b.start)
 
     load_p.wait()
@@ -550,13 +551,13 @@
         g_r[:, LOW, :] += got_c[:, LOW, :]
 
     when(me.has_u & me.has_r, add_c_low)
-    when(me.has_r & (tx != xh - 1), ra.start)
-    when(x_from, ra_out.start)
+    when(me.has_r, ra.start)
 
     def add_c_high():
         cb.wait_recv()
         g_r[:, HIGH, :] += got_c[:, HIGH, :]
-        rb.start()
+        when(tx != xh - 1, rb.start)
+        when(x_from, rb_out.start)
 
     when(me.has_r & me.odd, add_c_high)
 
@@ -572,11 +573,11 @@
     part[0:128, :] = own_rows(sums, 128, x) + rows_a[0] + rows_a[1] + rows_a[2]
     sent_y = share(4, 1, peers_y, part, rows_b, 32, y)
 
-    def pass_ra():
-        ra_out.wait_recv()
-        ra_fwd.start()
-
-    when(x_via, pass_ra)
+    def pass_rb():
+        rb_out.wait_recv()
+        rb_fwd.start()
+
+    when(x_via, pass_rb)
     for out_l, fwd in zip(l1_out, l1_fwd):
 
         def pass_l1():
@@ -662,7 +663,7 @@
         rb.wait_send()
 
     when(me.has_r, sent_r)
-    when(x_via, ra_fwd.wait_send)
+    when(x_via, rb_fwd.wait_send)
 
     def sent_fwd():
         l1_fwd[0].wait_send()

time: 211 us -> 211 us (level)
  no operation moved by 1% of the time
where the time goes in v3:
time: 211 us; the launch traced here: 210 us
  Pallas kernels  202 us (96%)
  local copies, waits for them, and re-layouts  7.6 us (4%)
    pallas_call x1, Pallas kernels, give(): pl.pallas_call(give_kernel, out_shape=[jax.ShapeDtypeStruct((2, M, 2 * M)...  102 us
    pallas_call x1, Pallas kernels, slots(): pl.pallas_call(slots_kernel, out_shape=[jax.ShapeDtypeStruct((2, 2 * M, 3...  100 us
    unnamed x5, local copies, waits for them, and re-layouts  7.6 us

profile of v3, /device:TPU:125, one launch (start us, length us, event | category | flops | bytes accessed | tf_op | source)
XLA Modules:
  0.0 210.4 jit_solution(14627938232145969017)
XLA Ops:
  0.6 1.3 copy.12.off
  2.0 100.3 %fetch_and_slots.1 = (f32[2,1024,1536]{2,1,0:T(8,128)}, f32[2,512,512]{2,1,0:T(8,128)}) custom-call(s32[3,2]{1,0:T(4,128)} %copy.12.off, s32[3]{0:T(128)} %live.1, f32[2,512,1024]{2,1,0:T(8,128)} %tile.1, f32[3,512,512]{2,1,0:T(8,128)} %amp.1, f32[2,512,512]{2,1,0:T(8,128)} %pup.1, bf16[4,256,256]{2,1,0:T(8,128)(2,1)} %constant.10.clone.mh, ...), custom_call_target="tpu_custom_call" | custom-call | tf_op jit(solution)/shard_map/fetch_and_slots/pallas_call | solution.py:387
  102.2 101.9 %give_back.1 = (f32[2,512,1024]{2,1,0:T(8,128)}, f32[2,512,512]{2,1,0:T(8,128)}) custom-call(f32[2,1024,1536]{2,1,0:T(8,128)} %get-tuple-element.4.grads, f32[2,512,512]{2,1,0:T(8,128)} %get-tuple-element.5.dpup), custom_call_target="tpu_custom_call" | custom-call | tf_op jit(solution)/shard_map/give_back/pallas_call | solution.py:677
  204.2 0.0 copy-start
  204.2 4.9 %copy.15 = f32[2,512,1024]{2,1,0:T(8,128)} copy(f32[2,512,1024]{2,1,0:T(8,128)} %get-tuple-element.8) | data formatting | bytes 8388608
  209.1 0.0 copy-done
  209.1 1.3 copy.16
Async XLA Ops:
  204.2 4.9 %copy-start = (f32[2,512,512]{2,1,0:T(8,128)S(1)}, f32[2,512,512]{2,1,0:T(8,128)}, u32[]{:S(2)}) copy-start(f32[2,512,512]{2,1,0:T(8,128)} %get-tuple-element.9) | copy-start | bytes 6291460
